TPU v7x, 256 devices: a whole 4x4x8 slice. The times are simulated.
256 devices in a mesh: dp: 16 (over z, core), tensor: 16 (over y, x).
Axes of the slice: x: 4, y: 4, z: 8, core: 2. Of those that a mesh axis runs over, the one named last changes fastest.
Arguments:
- grads: bfloat16 [16, 4096, 14336], P('dp', 'tensor'), as said below
- basis: float32 [4096, 512], P('tensor'), as said below
- weight: float32 [4096, 14336], P('tensor', 'dp'), may hold values from -6 to 6
- first_moment: float32 [512, 14336], P('tensor', 'dp'), may hold values from -0.6 to 0.6
- second_moment: float32 [512, 14336], P('tensor', 'dp'), may hold values from 0.01 to 0.1
Outputs:
- new_weight: float32 [4096, 14336], P('tensor', 'dp')
- new_first: float32 [512, 14336], P('tensor', 'dp')
- new_second: float32 [512, 14336], P('tensor', 'dp')
Inputs may be any that keep to these rules, and one draw needn't show every extreme that they name: `grads`: each member's gradient: entries of order tens, with magnitudes up to some 2,600. A dense basis with entries of order 1 / sqrt(4096).
All inputs are finite; a program needn't handle non-finite values.
Results may differ from a plain program's by a relative error of at most 0.0003.
Values sent between devices are 32-bit elements; how exact they have to be, the bound alone decides.
A program may use at most 128 MiB of HBM per device.

v0:
```python
import jax
import jax.numpy as jnp
from jax import lax
from jax.sharding import PartitionSpec as P

FFW = 14336
R = 512
STEP = 10


def body(grads, basis, weight, first_moment, second_moment):
    local = grads[0]
    reduced = lax.psum_scatter(local.astype(jnp.float32), "dp", scatter_dimension=1, tiled=True)
    basis_cols = basis
    projected = lax.psum_scatter(
        lax.dot_general(
            basis_cols,
            reduced,
            (((0,), (0,)), ((), ())),
            precision=lax.Precision.HIGHEST,
            preferred_element_type=jnp.float32,
        ),
        "tensor",
        scatter_dimension=0,
        tiled=True,
    )
    squares = lax.psum(jnp.sum(projected * projected), ("dp", "tensor"))
    limit = 0.25 * (R * FFW) ** 0.5
    factor = jnp.minimum(jnp.float32(1.0), limit / (jnp.sqrt(squares) + 1e-06))
    clipped = factor * projected
    new_first = 0.9 * first_moment + 0.1 * clipped
    new_second = 0.95 * second_moment + 0.05 * clipped * clipped
    direction = new_first / (1.0 - 0.9**STEP) / (jnp.sqrt(new_second / (1.0 - 0.95**STEP)) + 1e-08)
    basis_cols = basis
    delta = jnp.dot(
        basis_cols,
        lax.all_gather(direction, "tensor", axis=0, tiled=True),
        precision=lax.Precision.HIGHEST,
        preferred_element_type=jnp.float32,
    )
    new_weight = weight - 0.5 * delta
    return (new_weight, new_first, new_second)


def solution(mesh):
    in_specs = (
        P("dp", "tensor", None),
        P("tensor", None),
        P("tensor", "dp"),
        P("tensor", "dp"),
        P("tensor", "dp"),
    )
    out_specs = (P("tensor", "dp"), P("tensor", "dp"), P("tensor", "dp"))
    return jax.shard_map(body, mesh=mesh, in_specs=in_specs, out_specs=out_specs, check_vma=False)
```

profile of v0, /device:TPU:4, one launch (start us, length us, event | category | flops | bytes accessed | tf_op | source)
XLA Modules:
  0.0 330.0 jit_solution(2912742182797540016)
XLA Ops:
  7.2 0.0 copy-start
  7.2 0.0 reduce-scatter.3.cloned.1.call-start
  7.2 10.1 %bitcast_convert_fusion = f32[256,14336]{1,0:T(8,128)} fusion(bf16[1,256,14336]{2,1,0:T(8,128)(2,1)} %param.5), kind=kLoop, calls=%fused_computation | loop fusion | flops 3670016 | bytes 22020096 | tf_op jit(solution)/shard_map/convert_element_type | solution.py:13
  17.3 0.0 reduce-scatter.3.cloned.1.call-update
  17.3 0.0 copy-start.2
  17.3 0.0 copy-start.3
  17.4 0.0 reduce-scatter.5.cloned.1.call-start
  17.4 92.9 %reduce-scatter.3.cloned.1.call-done = f32[256,896]{1,0:T(8,128)} async-done(((f32[256,14336]{1,0:T(8,128)}), f32[256,896]{1,0:T(8,128)}) %reduce-scatter.3.cloned.1.call-update) | async-done | bytes 917520 | tf_op jit(solution)/shard_map/reduce_scatter | solution.py:13
  110.3 0.0 copy-done
  110.3 4.3 %fusion.4 = f32[512,896]{1,0:T(8,128)} fusion(f32[256,512]{1,0:T(8,128)S(1)} %copy-done, f32[256,896]{1,0:T(8,128)} %reduce-scatter.3.cloned.1.call-done), kind=kOutput, calls=%fused_computation.9 | convolution fusion | flops 1409286144 | bytes 3276800 | tf_op jit(solution)/shard_map/dot_general | solution.py:16
  114.6 0.0 copy-start.1
  114.6 0.0 reduce-scatter.5.cloned.1.call-update
  114.6 0.0 all-gather.2.cloned.1.call-start
  114.7 77.7 %reduce-scatter.5.cloned.1.call-done = f32[32,896]{1,0:T(8,128)} async-done(((f32[512,896]{1,0:T(8,128)}), f32[32,896]{1,0:T(8,128)}) %reduce-scatter.5.cloned.1.call-update) | async-done | bytes 114704 | tf_op jit(solution)/shard_map/reduce_scatter | solution.py:15
  192.4 1.5 multiply_reduce_fusion
  193.9 74.4 %psum.7 = f32[]{:T(128)} all-reduce(f32[]{:T(128)} %multiply_reduce_fusion), channel_id=1, replica_groups=mesh['dp'=16,'tensor'=16] {'dp','tensor'}, use_global_device_ids=true, to_apply=%region_3.0 | all-reduce | flops 1 | bytes 8 | tf_op jit(solution)/shard_map/psum | solution.py:27
  269.0 0.0 copy-done.2
  269.1 0.0 copy-done.3
  269.1 1.7 add_divide_fusion
  270.7 0.0 all-gather.2.cloned.1.call-update
  270.7 0.0 copy-done.1
  270.8 0.3 copy.8
  271.1 46.7 %all-gather.2.cloned.1.call-done = f32[512,896]{1,0:T(8,128)} async-done(((f32[32,896]{1,0:T(8,128)}), f32[512,896]{1,0:T(8,128)}) %all-gather.2.cloned.1.call-update) | async-done | bytes 1835024 | tf_op jit(solution)/shard_map/all_gather | solution.py:37
  317.7 4.5 %fusion.1 = f32[256,896]{0,1:T(8,128)S(1)} fusion(f32[256,896]{0,1:T(8,128)S(1)} %copy.8, f32[512,896]{1,0:T(8,128)} %all-gather.2.cloned.1.call-done, f32[256,512]{1,0:T(8,128)S(1)} %copy-done), kind=kOutput, calls=%fused_computation.3 | convolution fusion | flops 1409744896 | bytes 4194304 | tf_op jit(solution)/shard_map/dot_general | solution.py:35
  322.2 1.2 copy.9
Async XLA Ops:
  7.2 103.2 %copy-start = (f32[256,512]{1,0:T(8,128)S(1)}, f32[256,512]{1,0:T(8,128)}, u32[]{:S(2)}) copy-start(f32[256,512]{1,0:T(8,128)} %param.6) | copy-start | bytes 1572868
  7.2 103.1 %reduce-scatter.3.cloned.1.call-start = ((), (), s32[]{:S(2)}) async-start(), calls=%async_computation.2 | async-start | bytes 15597568 | tf_op jit(solution)/shard_map/reduce_scatter | solution.py:13
  17.3 251.7 %copy-start.2 = (f32[32,896]{1,0:T(8,128)S(1)}, f32[32,896]{1,0:T(8,128)}, u32[]{:S(2)}) copy-start(f32[32,896]{1,0:T(8,128)} %param.8) | copy-start | bytes 344068
  17.3 251.7 %copy-start.3 = (f32[32,896]{1,0:T(8,128)S(1)}, f32[32,896]{1,0:T(8,128)}, u32[]{:S(2)}) copy-start(f32[32,896]{1,0:T(8,128)} %param.9) | copy-start | bytes 344068
  17.4 175.0 %reduce-scatter.5.cloned.1.call-start = ((), (), s32[]{:S(2)}) async-start(), calls=%async_computation.3 | async-start | bytes 1949696 | tf_op jit(solution)/shard_map/reduce_scatter | solution.py:15
  114.6 156.2 %copy-start.1 = (f32[256,896]{1,0:T(8,128)S(1)}, f32[256,896]{1,0:T(8,128)}, u32[]{:S(2)}) copy-start(f32[256,896]{1,0:T(8,128)} %param.7) | copy-start | bytes 2752516
  114.6 203.1 %all-gather.2.cloned.1.call-start = ((), (), s32[]{:S(2)}) async-start(), calls=%async_computation.4 | async-start | bytes 1949696 | tf_op jit(solution)/shard_map/all_gather | solution.py:37
Sparse Core Ops, SparseCore 0:
  17.4 92.8 reduce-scatter.2
  114.7 77.6 reduce-scatter.4
  270.9 46.8 all-gather.1
where the time goes:
time: 331 us; the launch traced here: 330 us
  waiting for transfers between devices  217 us (66%)
  blocking collectives  74.4 us (22%)
  between operations  14.5 us (4%)
  other arithmetic  13.3 us (4%)
  matrix products  8.8 us (3%)
    reduce_scatter x1, waiting for transfers between devices, body(): lax.psum_scatter(local.astype(jnp.float32), 'dp', scatter_dimension=1, ti...  92.9 us
    reduce_scatter x1, waiting for transfers between devices, body(): lax.psum_scatter(lax.dot_general(basis_cols, reduced, (((0,), (0,)), ((),...  77.7 us
    psum x1, blocking collectives, body(): squares = lax.psum(jnp.sum(projected * projected), ('dp', 'tensor'))  74.4 us
    all_gather x1, waiting for transfers between devices, body(): lax.all_gather(direction, 'tensor', axis=0, tiled=True)  46.7 us
    convert_element_type x1, other arithmetic, body(): local.astype(jnp.float32)  10.1 us
  transfers between devices with their start and end apart: 3, of which 3 were waited for; matrix products, arithmetic and copies ran while one was open for 0% of the time, Pallas kernels for 0%

commit v1 on v0

v1 whole, which is shorter than its diff:
```python
import jax
import jax.numpy as jnp
from jax import lax
from jax.experimental import pallas as pl
from jax.experimental.pallas import tpu as pltpu
from jax.sharding import PartitionSpec as P

FFW = 14336
R = 512
STEP = 10
OWN = 896
LANE = 128
ROWS = 256
NZ = 8
NA = 4
NB = 3
MESH = pl.DeviceIdType.MESH
F32 = jnp.float32
BF16 = jnp.bfloat16


def split(x):
    hi = x.astype(BF16)
    return hi, (x - hi.astype(F32)).astype(BF16)


def dot3(ah, al, bh, bl):
    def mm(a, b):
        return jnp.dot(a, b, preferred_element_type=F32)

    return mm(ah, bh) + (mm(ah, bl) + mm(al, bh))


def kernel(
    g_ref, basis_ref, weight_ref, first_ref, second_ref,
    out_ref, out_first_ref, out_second_ref,
    ga, gb, cs, cr, zr, pb, rb1, rb2, rb3, rb4, qr, pa, ar,
    fin, ssq1, ssq2, dirs, wbuf, m1, m2, bbuf, bth, btl, bh, bl,
    gsem, lsem, csend, crecv, zsend, zrecv, asend, arecv,
    bsend, brecv, qsend, qrecv, nsend, nrecv, dsend, drecv,
):
    d = lax.axis_index("dp")
    t = lax.axis_index("tensor")
    z, c = d // 2, d % 2
    y, x = t // 4, t % 4

    def at_z(k):
        return (((z + k + NZ) % NZ) * 2 + c, t)

    def at_x(k):
        return (d, y * 4 + (x + k + 4) % 4)

    def at_y(k):
        return (d, ((y + k + 4) % 4) * 4 + x)

    partner = (z * 2 + 1 - c, t)

    def gload(group, which, start):
        core = c if which == 0 else 1 - c
        if group < 2:
            buf, lo, width = ga.at[which, group], 256 * group, 256
        else:
            buf, lo, width = gb.at[which], NA * LANE, NB * LANE
        sem = gsem.at[group, which]
        if not start:
            pltpu.make_async_copy(buf, buf, sem).wait()
            return

        def one(k, _):
            col = pl.multiple_of(OWN * (2 * k + core) + lo, LANE)
            pltpu.make_async_copy(g_ref.at[:, pl.ds(col, width)], buf.at[k], sem).start()
            return 0

        lax.fori_loop(0, NZ, one, 0)

    small = [
        pltpu.make_async_copy(basis_ref, bbuf, lsem.at[0]),
        pltpu.make_async_copy(first_ref, m1, lsem.at[1]),
        pltpu.make_async_copy(second_ref, m2, lsem.at[2]),
        pltpu.make_async_copy(weight_ref, wbuf, lsem.at[3]),
    ]
    gload(0, 1, True)
    gload(0, 0, True)
    small[0].start()
    gload(2, 1, True)
    gload(2, 0, True)
    gload(1, 1, True)
    gload(1, 0, True)
    for cp in small[1:]:
        cp.start()

    barrier = pltpu.get_barrier_semaphore()

    def greet(k, _):
        pl.semaphore_signal(barrier, 1, device_id=((d + k) % 16, t), device_id_type=MESH)
        pl.semaphore_signal(barrier, 1, device_id=(d, (t + k) % 16), device_id_type=MESH)
        return 0

    lax.fori_loop(1, 16, greet, 0)

    pending = []

    def remote(src, dst, ssem, rsem, dev):
        cp = pltpu.make_async_remote_copy(
            src_ref=src, dst_ref=dst, send_sem=ssem, recv_sem=rsem,
            device_id=dev, device_id_type=MESH,
        )
        cp.start()
        pending.append(cp)
        return cp

    loaded = set()

    def grad(j, which, k):
        if j < NA:
            return ga[which, j // 2, k, :, (j % 2) * LANE:(j % 2 + 1) * LANE].astype(F32)
        return gb[which, k, :, (j - NA) * LANE:(j - NA + 1) * LANE].astype(F32)

    def need(j, which):
        group = j // 2 if j < NA else 2
        if (group, which) not in loaded:
            loaded.add((group, which))
            gload(group, which, False)

    core = {}

    def cast(j):
        need(j, 1)

        def one(k, _):
            cs[j, k] = grad(j, 1, k)
            return 0

        lax.fori_loop(0, NZ, one, 0)

    def exchange(j):
        core[j] = remote(cs.at[j], cr.at[j], csend.at[j], crecv.at[j], partner)

    def stage(j):
        cast(j)
        exchange(j)

    def block(k):
        return (z + k + 2 * NZ) % NZ

    az = {}

    def a_send(j, s):
        if s == 1:
            far = block(4)
            az[j, 0, 1] = remote(
                cr.at[j, far, 0:128], zr.at[j, 0, 0, 0:128],
                zsend.at[j, 0, 0], zrecv.at[j, 0, 0], at_z(1))
            az[j, 1, 1] = remote(
                cr.at[j, far, 128:256], zr.at[j, 1, 0, 0:128],
                zsend.at[j, 1, 0], zrecv.at[j, 1, 0], at_z(-1))
            return
        for side, sign in ((0, 1), (1, -1)):
            dest = block(sign * (5 - s))
            az[j, side, s - 1].wait_recv()
            if s == 2:
                rows = pl.ds(128 * side, 128)
                cr[j, dest, rows] = cr[j, dest, rows] + zr[j, side, 0, 0:128]
            else:
                cr[j, dest] = cr[j, dest] + zr[j, side, s - 2]
            az[j, side, s] = remote(
                cr.at[j, dest], zr.at[j, side, s - 1],
                zsend.at[j, side, s - 1], zrecv.at[j, side, s - 1], at_z(sign))

    def a1(j):
        need(j, 0)
        core[j].wait_recv()

        def one(k, _):
            cr[j, k] = cr[j, k] + grad(j, 0, k)
            return 0

        lax.fori_loop(0, NZ, one, 0)
        a_send(j, 1)

    def a5(j):
        az[j, 0, 4].wait_recv()
        az[j, 1, 4].wait_recv()
        total = cr[j, z] + zr[j, 0, 3] + zr[j, 1, 3]
        hi, lo = split(total)
        pa[j] = dot3(bth[...], btl[...], hi, lo).reshape(16, 32, LANE)

        def one(k, _):
            to = (t + k) % 16
            pltpu.make_async_remote_copy(
                src_ref=pa.at[j, to], dst_ref=ar.at[j, k - 1],
                send_sem=asend.at[j], recv_sem=arecv.at[j],
                device_id=(d, to), device_id_type=MESH).start()
            return 0

        lax.fori_loop(1, 16, one, 0)

    def wait_bytes(ref, sem):
        pltpu.make_async_copy(ref, ref, sem).wait()

    def a6(j):
        wait_bytes(ar.at[j], arecv.at[j])
        fin[:, j * LANE:(j + 1) * LANE] = pa[j, t] + jnp.sum(ar[j], axis=0)

    bx = {}

    def piece(j, h, stage_no, k, cols):
        lane = pl.ds(512 * h + cols[0], cols[1])
        if stage_no == 0:
            if h == 0:
                return pb.at[j, :, (x + k + 4) % 4, :, lane]
            return pb.at[j, (y + k + 4) % 4, :, :, lane]
        if h == 0:
            return pb.at[j, (y + k + 4) % 4, x, :, lane]
        return pb.at[j, y, (x + k + 4) % 4, :, lane]

    def toward(h, stage_no, k):
        return at_x(k) if (h + stage_no) % 2 == 0 else at_y(k)

    def b_first(j, stage_no):
        buf = rb1 if stage_no == 0 else rb3
        for h in (0, 1):
            for side, sign in ((0, 1), (1, -1)):
                bx[j, h, side, stage_no, 0] = remote(
                    piece(j, h, stage_no, 2, (256 * side, 256)), buf.at[j, h, side],
                    bsend.at[j, h, side, 2 * stage_no], brecv.at[j, h, side, 2 * stage_no],
                    toward(h, stage_no, sign))

    def b_second(j, stage_no):
        got, buf = (rb1, rb2) if stage_no == 0 else (rb3, rb4)
        for h in (0, 1):
            for side, sign in ((0, 1), (1, -1)):
                bx[j, h, side, stage_no, 0].wait_recv()
                part = piece(j, h, stage_no, sign, (256 * side, 256))
                part[...] = part[...] + got[j, h, side]
                bx[j, h, side, stage_no, 1] = remote(
                    piece(j, h, stage_no, sign, (0, 512)), buf.at[j, h, side],
                    bsend.at[j, h, side, 2 * stage_no + 1], brecv.at[j, h, side, 2 * stage_no + 1],
                    toward(h, stage_no, sign))

    def b_close(j, stage_no):
        buf = rb2 if stage_no == 0 else rb4
        for h in (0, 1):
            bx[j, h, 0, stage_no, 1].wait_recv()
            bx[j, h, 1, stage_no, 1].wait_recv()
            part = piece(j, h, stage_no, 0, (0, 512))
            part[...] = part[...] + (buf[j, h, 0] + buf[j, h, 1])

    def b1(j):
        n = NA + j
        need(n, 0)
        core[n].wait_recv()

        def one(q, _):
            total = jnp.concatenate(
                [cr[n, 2 * q] + grad(n, 0, 2 * q), cr[n, 2 * q + 1] + grad(n, 0, 2 * q + 1)], axis=1)
            hi, lo = split(total)
            cols = pl.ds(pl.multiple_of(q * 256, 256), 256)
            pb[j, :, :, :, cols] = dot3(bth[...], btl[...], hi, lo).reshape(4, 4, 32, 256)
            return 0

        lax.fori_loop(0, 4, one, 0)
        b_first(j, 0)

    def b3(j):
        b_close(j, 0)
        b_first(j, 1)

    def b5(j):
        b_close(j, 1)

        def one(k, _):
            to = (z + k) % NZ
            cols = pl.ds(pl.multiple_of(to * LANE, LANE), LANE)
            pltpu.make_async_remote_copy(
                src_ref=pb.at[j, y, x, :, cols], dst_ref=qr.at[j, k - 1],
                send_sem=qsend.at[j], recv_sem=qrecv.at[j],
                device_id=(to * 2 + c, t), device_id_type=MESH).start()
            return 0

        lax.fori_loop(1, NZ, one, 0)

    def b6(j):
        wait_bytes(qr.at[j], qrecv.at[j])
        cols = pl.ds(pl.multiple_of(z * LANE, LANE), LANE)
        n = NA + j
        fin[:, n * LANE:(n + 1) * LANE] = pb[j, y, x, :, cols] + jnp.sum(qr[j], axis=0)

    def a2(j):
        a_send(j, 2)

    def a3(j):
        a_send(j, 3)

    def a4(j):
        a_send(j, 4)

    def b2(j):
        b_second(j, 0)

    def b4(j):
        b_second(j, 1)

    first_tiles = (0, 1, 4)
    for j in first_tiles:
        cast(j)
    small[0].wait()
    b = bbuf[...]
    hi, lo = split(b)
    bh[...] = hi
    bl[...] = lo
    hi, lo = split(b.T)
    bth[...] = hi
    btl[...] = lo
    pl.semaphore_wait(barrier, 30)
    for j in first_tiles:
        exchange(j)
    order = (
        (a1, 0), (a1, 1), (stage, 5), (b1, 0), (stage, 6), (stage, 2), (stage, 3),
        (a2, 0), (a2, 1), (b1, 1), (b2, 0), (a3, 0), (a3, 1), (b1, 2), (a4, 0), (b2, 1), (a4, 1),
        (b3, 0), (a1, 2), (a1, 3), (b4, 0), (a5, 0), (b2, 2), (a5, 1), (b5, 0), (a2, 2), (b3, 1), (a2, 3),
        (b4, 1), (a3, 2), (b3, 2), (a3, 3), (b5, 1), (b4, 2), (a4, 2), (b5, 2), (a4, 3),
        (a6, 0), (a6, 1), (b6, 0), (b6, 1), (a5, 2), (b6, 2), (a5, 3), (a6, 2), (a6, 3),
    )
    for step, j in order:
        step(j)

    acc = jnp.zeros((8, LANE), F32)
    for r in range(4):
        for j in range(7):
            v = fin[8 * r:8 * r + 8, LANE * j:LANE * (j + 1)]
            acc = acc + v * v

    def spread(buf, n, dev):
        def one(k, _):
            pltpu.make_async_remote_copy(
                src_ref=buf.at[15], dst_ref=buf.at[k - 1],
                send_sem=nsend.at[n], recv_sem=nrecv.at[n],
                device_id=dev(k), device_id_type=MESH).start()
            return 0

        lax.fori_loop(1, 16, one, 0)

    ssq1[15] = acc
    spread(ssq1, 0, lambda k: ((d + k) % 16, t))
    for cp in pending:
        cp.wait_send()
    pending.clear()
    for j in range(NA):
        wait_bytes(ar.at[j], asend.at[j])
    for j in range(NB):
        wait_bytes(qr.at[j], qsend.at[j])
    small[1].wait()
    small[2].wait()
    small[3].wait()
    wait_bytes(ssq1.at[0:15], nrecv.at[0])
    ssq2[15] = jnp.sum(ssq1[...], axis=0)
    spread(ssq2, 1, lambda k: (d, (t + k) % 16))
    wait_bytes(ssq1.at[0:15], nsend.at[0])
    wait_bytes(ssq2.at[0:15], nrecv.at[1])
    squares = jnp.sum(jnp.sum(ssq2[...], axis=0), axis=0, keepdims=True)
    squares = jnp.sum(squares, axis=1, keepdims=True)
    limit = 0.25 * (R * FFW) ** 0.5
    factor = jnp.minimum(jnp.float32(1.0), limit / (jnp.sqrt(squares) + 1e-06))

    clipped = factor * fin[...]
    new_first = 0.9 * m1[...] + 0.1 * clipped
    new_second = 0.95 * m2[...] + 0.05 * clipped * clipped
    m1[...] = new_first
    m2[...] = new_second
    dirs[y, x] = new_first / (1.0 - 0.9**STEP) / (jnp.sqrt(new_second / (1.0 - 0.95**STEP)) + 1e-08)

    span = ((0, 512), (512, 384))
    cut = (((0, 256), (256, 256)), ((512, 256), (768, 128)))
    dx = {}

    def rows_of(h, ring, k, cols):
        lane = pl.ds(*cols)
        if ring == 0:
            if h == 0:
                return dirs.at[y, (x + k + 4) % 4, :, lane]
            return dirs.at[(y + k + 4) % 4, x, :, lane]
        if h == 0:
            return dirs.at[(y + k + 4) % 4, :, :, lane]
        return dirs.at[:, (x + k + 4) % 4, :, lane]

    def d_send(h, ring, hop):
        for side, sign in ((0, 1), (1, -1)):
            if hop == 0:
                ref = rows_of(h, ring, 0, span[h])
            else:
                dx[h, ring, 0, side].wait_recv()
                ref = rows_of(h, ring, -sign, cut[h][side])
            n = 2 * ring + hop
            dx[h, ring, hop, side] = remote(
                ref, ref, dsend.at[h, n, side], drecv.at[h, n, side], toward(h, ring, sign))

    def d_wait(h, ring):
        dx[h, ring, 1, 0].wait_recv()
        dx[h, ring, 1, 1].wait_recv()

    d_send(0, 0, 0)
    d_send(1, 0, 0)
    outs = [
        pltpu.make_async_copy(m1, out_first_ref, lsem.at[1]),
        pltpu.make_async_copy(m2, out_second_ref, lsem.at[2]),
    ]
    for cp in outs:
        cp.start()
    d_send(0, 0, 1)
    d_send(1, 0, 1)
    d_wait(0, 0)
    d_send(0, 1, 0)
    d_wait(1, 0)
    d_send(1, 1, 0)
    d_send(0, 1, 1)
    d_send(1, 1, 1)
    wait_bytes(ssq2.at[0:15], nsend.at[1])
    for h in (0, 1):
        d_wait(h, 1)
        for n, (lo_col, width) in enumerate(cut[h]):
            cols = slice(lo_col, lo_col + width)
            hi, lo = split(dirs[:, :, :, cols].reshape(R, width))
            wbuf[:, cols] = wbuf[:, cols] - 0.5 * dot3(bh[...], bl[...], hi, lo)
            cp = pltpu.make_async_copy(wbuf.at[:, cols], out_ref.at[:, cols], lsem.at[3 + 2 * h + n])
            cp.start()
            outs.append(cp)
    for cp in pending:
        cp.wait_send()
    for cp in outs:
        cp.wait()


def body(grads, basis, weight, first_moment, second_moment):
    dma = pltpu.SemaphoreType.DMA
    vmem = pltpu.VMEM
    return pl.pallas_call(
        kernel,
        out_shape=(
            jax.ShapeDtypeStruct((ROWS, OWN), F32),
            jax.ShapeDtypeStruct((32, OWN), F32),
            jax.ShapeDtypeStruct((32, OWN), F32),
        ),
        in_specs=[pl.BlockSpec(memory_space=pl.ANY)] * 5,
        out_specs=[pl.BlockSpec(memory_space=pl.ANY)] * 3,
        scratch_shapes=[
            vmem((2, 2, NZ, ROWS, 256), BF16),
            vmem((2, NZ, ROWS, NB * LANE), BF16),
            vmem((NA + NB, NZ, ROWS, LANE), F32),
            vmem((NA + NB, NZ, ROWS, LANE), F32),
            vmem((NA, 2, 4, ROWS, LANE), F32),
            vmem((NB, 4, 4, 32, 1024), F32),
            vmem((NB, 2, 2, 4, 32, 256), F32),
            vmem((NB, 2, 2, 4, 32, 512), F32),
            vmem((NB, 2, 2, 32, 256), F32),
            vmem((NB, 2, 2, 32, 512), F32),
            vmem((NB, NZ - 1, 32, LANE), F32),
            vmem((NA, 16, 32, LANE), F32),
            vmem((NA, 15, 32, LANE), F32),
            vmem((32, OWN), F32),
            vmem((16, 8, LANE), F32),
            vmem((16, 8, LANE), F32),
            vmem((4, 4, 32, OWN), F32),
            vmem((ROWS, OWN), F32),
            vmem((32, OWN), F32),
            vmem((32, OWN), F32),
            vmem((ROWS, R), F32),
            vmem((R, ROWS), BF16),
            vmem((R, ROWS), BF16),
            vmem((ROWS, R), BF16),
            vmem((ROWS, R), BF16),
            dma((3, 2)),
            dma((7,)),
            dma((NA + NB,)), dma((NA + NB,)),
            dma((NA, 2, 4)), dma((NA, 2, 4)),
            dma((NA,)), dma((NA,)),
            dma((NB, 2, 2, 4)), dma((NB, 2, 2, 4)),
            dma((NB,)), dma((NB,)),
            dma((2,)), dma((2,)),
            dma((2, 4, 2)), dma((2, 4, 2)),
        ],
        compiler_params=pltpu.CompilerParams(
            collective_id=0, has_side_effects=True, vmem_limit_bytes=62 * 2**20),
        name="galore_step",
    )(grads[0], basis, weight, first_moment, second_moment)


def solution(mesh):
    in_specs = (
        P("dp", "tensor", None),
        P("tensor", None),
        P("tensor", "dp"),
        P("tensor", "dp"),
        P("tensor", "dp"),
    )
    out_specs = (P("tensor", "dp"), P("tensor", "dp"), P("tensor", "dp"))
    return jax.shard_map(body, mesh=mesh, in_specs=in_specs, out_specs=out_specs, check_vma=False)
```

time: 331 us -> 119 us (0.36)
  waiting for transfers between devices: 217 us -> 0 us
  Pallas kernels: 0 us -> 111 us
  blocking collectives: 74.4 us -> 0 us
  between operations: 14.5 us -> 0.64 us
  other arithmetic: 13.3 us -> 0 us
  matrix products: 8.8 us -> 0 us
  local copies, waits for them, and re-layouts: 1.55 us -> 5.26 us
    reduce_scatter x2 -> x0, waiting for transfers between devices: 171 us -> none  [the longest x1 92.9 us: body(): lax.psum_scatter(local.astype(jnp.float32), 'dp', scatter_dimension=1, ti...]
    pallas_call x0 -> x1, Pallas kernels: none -> 111 us  [body(): pl.pallas_call(kernel, out_shape=(jax.ShapeDtypeStruct((ROWS, OWN), F32),...]
    psum x1 -> x0, blocking collectives: 74.4 us -> none  [body(): squares = lax.psum(jnp.sum(projected * projected), ('dp', 'tensor'))]
    all_gather x1 -> x0, waiting for transfers between devices: 46.7 us -> none  [body(): lax.all_gather(direction, 'tensor', axis=0, tiled=True)]
    convert_element_type x1 -> x0, other arithmetic: 10.1 us -> none  [body(): local.astype(jnp.float32)]
    dot_general x2 -> x0, matrix products: 8.8 us -> none  [the longest x1 4.52 us: body(): jnp.dot(basis_cols, lax.all_gather(direction, 'tensor', axis=0, tiled=Tru...]
    unnamed x10 -> x3, local copies, waits for them, and re-layouts: 1.55 us -> 5.26 us
  transfers between devices with their start and end apart: 3 -> 0, of which waited for: 3 -> 0; matrix products, arithmetic and copies ran while one was open for 0% -> 0% of each run, Pallas kernels for 0% -> 0%
where the time goes in v1:
time: 119 us; the launch traced here: 117 us
  Pallas kernels  111 us (93%)
  local copies, waits for them, and re-layouts  5.26 us (4%)
    pallas_call x1, Pallas kernels, body(): pl.pallas_call(kernel, out_shape=(jax.ShapeDtypeStruct((ROWS, OWN), F32),...  111 us
    unnamed x3, local copies, waits for them, and re-layouts  5.26 us

profile of v1, /device:TPU:4, one launch (start us, length us, event | category | flops | bytes accessed | tf_op | source)
XLA Modules:
  0.0 116.9 jit_solution(2417634016629764832)
XLA Ops:
  0.6 111.0 %galore_step.1 = (f32[256,896]{1,0:T(8,128)}, f32[32,896]{1,0:T(8,128)}, f32[32,896]{1,0:T(8,128)}) custom-call(bf16[256,14336]{1,0:T(8,128)(2,1)} %bitcast.1, f32[256,512]{1,0:T(8,128)} %basis_ref.1, f32[256,896]{1,0:T(8,128)} %weight_ref.1, f32[32,896]{1,0:T(8,128)} %first_ref.1, f32[32,896]{1,0:T(8,128)} %second_ref.1), custom_call_target="tpu_custom_call" | custom-call | tf_op jit(solution)/shard_map/galore_step/pallas_call | solution.py:437
  111.6 2.2 %copy.11 = f32[256,896]{1,0:T(8,128)} copy(f32[256,896]{1,0:T(8,128)} %get-tuple-element.6) | data formatting | bytes 1835008
  113.8 1.6 %copy.12 = f32[32,896]{1,0:T(8,128)} copy(f32[32,896]{1,0:T(8,128)} %get-tuple-element.7) | data formatting | bytes 229376
  115.3 1.6 %copy.13 = f32[32,896]{1,0:T(8,128)} copy(f32[32,896]{1,0:T(8,128)} %get-tuple-element.8) | data formatting | bytes 229376

commit v2 on v1

v2 whole, which is shorter than its diff:
```python
import jax
import jax.numpy as jnp
from jax import lax
from jax.experimental import pallas as pl
from jax.experimental.pallas import tpu as pltpu
from jax.sharding import PartitionSpec as P

FFW = 14336
R = 512
STEP = 10
OWN = 896
LANE = 128
ROWS = 256
NZ = 8
NA = 4
NB = 3
MESH = pl.DeviceIdType.MESH
F32 = jnp.float32
BF16 = jnp.bfloat16


def split(x):
    hi = x.astype(BF16)
    return hi, (x - hi.astype(F32)).astype(BF16)


def dot3(ah, al, bh, bl):
    def mm(a, b):
        return jnp.dot(a, b, preferred_element_type=F32)

    return mm(ah, bh) + (mm(ah, bl) + mm(al, bh))


def kernel(
    g_ref, basis_ref, first_ref, second_ref,
    out_ref, clipped_ref,
    ga, gb, cs, cr, zr, pb, rb1, rb2, rb3, rb4, qr, qz, pa, ah, hs, ar,
    fin, ssq1, ssq2, dirs, m1, m2, bbuf, bth, btl,
    gsem, lsem, fsend, frecv, csend, crecv, zsend, zrecv, asend, arecv,
    bsend, brecv, qsend, qrecv, hsend, hrecv, rsend, rrecv, nsend, nrecv, dsend, drecv,
):
    d = lax.axis_index("dp")
    t = lax.axis_index("tensor")
    z, c = d // 2, d % 2
    y, x = t // 4, t % 4

    def at_z(k):
        return (((z + k + NZ) % NZ) * 2 + c, t)

    def at_x(k):
        return (d, y * 4 + (x + k + 4) % 4)

    def at_y(k):
        return (d, ((y + k + 4) % 4) * 4 + x)

    partner = (z * 2 + 1 - c, t)

    def gload(group, which, start):
        core = c if which == 0 else 1 - c
        if group < 2:
            buf, lo, width = ga.at[which, group], 256 * group, 256
        else:
            buf, lo, width = gb.at[which], NA * LANE, NB * LANE
        sem = gsem.at[group, which]
        if not start:
            pltpu.make_async_copy(buf, buf, sem).wait()
            return

        def one(k, _):
            col = pl.multiple_of(OWN * (2 * ((z + 4 + k) % NZ) + core) + lo, LANE)
            pltpu.make_async_copy(g_ref.at[:, pl.ds(col, width)], buf.at[k], sem).start()
            return 0

        lax.fori_loop(0, NZ, one, 0)

    small = [
        pltpu.make_async_copy(basis_ref, bbuf, lsem.at[0]),
        pltpu.make_async_copy(first_ref, m1, lsem.at[1]),
        pltpu.make_async_copy(second_ref, m2, lsem.at[2]),
    ]
    gload(0, 1, True)
    gload(2, 1, True)
    gload(0, 0, True)
    small[0].start()
    gload(2, 0, True)
    gload(1, 1, True)
    gload(1, 0, True)
    for cp in small[1:]:
        cp.start()

    barrier = pltpu.get_barrier_semaphore()

    for to in (at_z(1), at_z(-1), at_x(1), at_x(-1), at_y(1), at_y(-1), partner):
        pl.semaphore_signal(barrier, 1, device_id=to, device_id_type=MESH)

    pending = []

    def remote(src, dst, ssem, rsem, dev):
        cp = pltpu.make_async_remote_copy(
            src_ref=src, dst_ref=dst, send_sem=ssem, recv_sem=rsem,
            device_id=dev, device_id_type=MESH,
        )
        cp.start()
        pending.append(cp)
        return cp

    loaded = set()

    def grad(j, which, k):
        if j < NA:
            return ga[which, j // 2, k, :, (j % 2) * LANE:(j % 2 + 1) * LANE].astype(F32)
        return gb[which, k, :, (j - NA) * LANE:(j - NA + 1) * LANE].astype(F32)

    def need(j, which):
        group = j // 2 if j < NA else 2
        if (group, which) not in loaded:
            loaded.add((group, which))
            gload(group, which, False)

    core = {}
    far = {}

    def cast(j, lo, hi):
        need(j, 1)

        def one(k, _):
            cs[j, k] = grad(j, 1, k)
            return 0

        lax.fori_loop(lo, hi, one, 0)

    def send_far(j):
        far[j] = remote(cs.at[j, 0], cr.at[j, 0], fsend.at[j], frecv.at[j], partner)

    def send_rest(j):
        core[j] = remote(cs.at[j, 1:NZ], cr.at[j, 1:NZ], csend.at[j], crecv.at[j], partner)

    def stage(j):
        cast(j, 0, NZ)
        if j < NA:
            send_far(j)
            send_rest(j)
        else:
            core[j] = remote(cs.at[j], cr.at[j], csend.at[j], crecv.at[j], partner)

    az = {}
    waited = set()

    def once(table, *keys):
        for key in keys:
            if (id(table), key) not in waited:
                waited.add((id(table), key))
                table[key].wait_recv()

    def a_send(j, s):
        for side, sign in ((0, 1), (1, -1)):
            dest = (4 + sign * (5 - s)) % NZ
            rows = pl.ds(0, ROWS)
            if s == 1:
                rows = pl.ds(128 * side, 128)
            elif s == 2:
                az[j, side, 1].wait_recv()
                half = pl.ds(128 * side, 128)
                cr[j, dest, half] = cr[j, dest, half] + zr[j, side, 0, 0:128]
            else:
                az[j, side, s - 1].wait_recv()
                cr[j, dest] = cr[j, dest] + zr[j, side, s - 2]
            to = zr.at[j, side, 0, 0:128] if s == 1 else zr.at[j, side, s - 1]
            az[j, side, s] = remote(
                cr.at[j, dest, rows], to,
                zsend.at[j, side, s - 1], zrecv.at[j, side, s - 1], at_z(sign))

    def a0(j):
        need(j, 0)
        far[j].wait_recv()
        cr[j, 0] = cr[j, 0] + grad(j, 0, 0)
        a_send(j, 1)

    def a1(j):
        core[j].wait_recv()

        def one(k, _):
            cr[j, k] = cr[j, k] + grad(j, 0, k)
            return 0

        lax.fori_loop(1, NZ, one, 0)

    def spread(src, dst, ssem, rsem, peers):
        for k, to in enumerate(peers):
            pltpu.make_async_remote_copy(
                src_ref=src(k + 1), dst_ref=dst.at[k], send_sem=ssem, recv_sem=rsem,
                device_id=to, device_id_type=MESH).start()

    def line(over_x):
        return [at_x(k) if over_x else at_y(k) for k in (1, 2, 3)]

    def a5(j):
        once(az, (j, 0, 4), (j, 1, 4))
        total = cr[j, 4] + zr[j, 0, 3] + zr[j, 1, 3]
        hi, lo = split(total)
        pa[j] = dot3(bth[...], btl[...], hi, lo).reshape(4, 4, 32, LANE)
        if j >= 2:
            spread(
                lambda k: pa.at[j, (t + k) % 16 // 4, (t + k) % 4], ar.at[j],
                asend.at[j], arecv.at[j], [(d, (t + k) % 16) for k in range(1, 16)])
        elif j == 0:
            spread(lambda k: pa.at[j, :, (x + k) % 4], ah.at[j], hsend.at[j], hrecv.at[j], line(True))
        else:
            spread(lambda k: pa.at[j, (y + k) % 4], ah.at[j], hsend.at[j], hrecv.at[j], line(False))

    def a7(j):
        wait_bytes(ah.at[j], hrecv.at[j])
        if j == 0:
            hs[j] = pa[j, :, x] + (ah[j, 0] + ah[j, 1] + ah[j, 2])
            spread(lambda k: hs.at[j, (y + k) % 4], ar.at[j], asend.at[j], arecv.at[j], line(False))
        else:
            hs[j] = pa[j, y] + (ah[j, 0] + ah[j, 1] + ah[j, 2])
            spread(lambda k: hs.at[j, (x + k) % 4], ar.at[j], asend.at[j], arecv.at[j], line(True))

    def wait_bytes(ref, sem):
        pltpu.make_async_copy(ref, ref, sem).wait()

    def a6(j):
        cols = slice(j * LANE, (j + 1) * LANE)
        if j >= 2:
            wait_bytes(ar.at[j], arecv.at[j])
            fin[:, cols] = pa[j, y, x] + jnp.sum(ar[j], axis=0)
        else:
            wait_bytes(ar.at[j, 0:3], arecv.at[j])
            fin[:, cols] = hs[j, y if j == 0 else x] + (ar[j, 0] + ar[j, 1] + ar[j, 2])

    bx = {}

    def piece(j, h, stage_no, k, cols):
        lane = pl.ds(512 * h + cols[0], cols[1])
        if stage_no == 0:
            if h == 0:
                return pb.at[j, :, (x + k + 4) % 4, :, lane]
            return pb.at[j, (y + k + 4) % 4, :, :, lane]
        if h == 0:
            return pb.at[j, (y + k + 4) % 4, x, :, lane]
        return pb.at[j, y, (x + k + 4) % 4, :, lane]

    def toward(h, stage_no, k):
        return at_x(k) if (h + stage_no) % 2 == 0 else at_y(k)

    def b_first(j, stage_no):
        buf = rb1 if stage_no == 0 else rb3
        for h in (0, 1):
            for side, sign in ((0, 1), (1, -1)):
                bx[j, h, side, stage_no, 0] = remote(
                    piece(j, h, stage_no, 2, (256 * side, 256)), buf.at[j, h, side],
                    bsend.at[j, h, side, 2 * stage_no], brecv.at[j, h, side, 2 * stage_no],
                    toward(h, stage_no, sign))

    def b_second(j, stage_no):
        got, buf = (rb1, rb2) if stage_no == 0 else (rb3, rb4)
        for h in (0, 1):
            for side, sign in ((0, 1), (1, -1)):
                bx[j, h, side, stage_no, 0].wait_recv()
                part = piece(j, h, stage_no, sign, (256 * side, 256))
                part[...] = part[...] + got[j, h, side]
                bx[j, h, side, stage_no, 1] = remote(
                    piece(j, h, stage_no, sign, (0, 512)), buf.at[j, h, side],
                    bsend.at[j, h, side, 2 * stage_no + 1], brecv.at[j, h, side, 2 * stage_no + 1],
                    toward(h, stage_no, sign))

    def b_close(j, stage_no):
        buf = rb2 if stage_no == 0 else rb4
        for h in (0, 1):
            once(bx, (j, h, 0, stage_no, 1), (j, h, 1, stage_no, 1))
            part = piece(j, h, stage_no, 0, (0, 512))
            part[...] = part[...] + (buf[j, h, 0] + buf[j, h, 1])

    def b1(j):
        n = NA + j
        need(n, 0)
        core[n].wait_recv()

        def one(q, _):
            total = jnp.concatenate(
                [cr[n, 2 * q] + grad(n, 0, 2 * q), cr[n, 2 * q + 1] + grad(n, 0, 2 * q + 1)], axis=1)
            hi, lo = split(total)
            cols = pl.ds(pl.multiple_of(q * 256, 256), 256)
            pb[j, :, :, :, cols] = dot3(bth[...], btl[...], hi, lo).reshape(4, 4, 32, 256)
            return 0

        lax.fori_loop(0, 4, one, 0)
        b_first(j, 0)

    def b3(j):
        b_close(j, 0)
        b_first(j, 1)

    rx = {}

    def r_send(j, s):
        for side, sign in ((0, 1), (1, -1)):
            dest = (4 + sign * (5 - s)) % NZ
            col = slice(LANE * dest, LANE * (dest + 1))
            rows = slice(0, 32)
            if s <= 2:
                half = slice(16 * side, 16 * side + 16)
            if s == 1:
                rows = half
            else:
                rx[j, side, s - 1].wait_recv()
                if s == 2:
                    pb[j, y, x, half, col] = pb[j, y, x, half, col] + qz[side, 0, 0:16]
                else:
                    pb[j, y, x, :, col] = pb[j, y, x, :, col] + qz[side, s - 2]
            to = qz.at[side, 0, 0:16] if s == 1 else qz.at[side, s - 1]
            rx[j, side, s] = remote(
                pb.at[j, y, x, rows, col], to,
                rsend.at[side, s - 1], rrecv.at[side, s - 1], at_z(sign))

    def b5(j):
        b_close(j, 1)
        if j == 0:
            r_send(j, 1)
            return

        def block(k):
            col = LANE * ((4 + k) % NZ)
            return pb.at[j, y, x, :, col:col + LANE]

        spread(block, qr.at[j], qsend.at[j], qrecv.at[j], [at_z(k) for k in range(1, NZ)])

    def b6(j):
        n = NA + j
        own = pb[j, y, x, :, 4 * LANE:5 * LANE]
        if j == 0:
            rx[j, 0, 4].wait_recv()
            rx[j, 1, 4].wait_recv()
            fin[:, n * LANE:(n + 1) * LANE] = own + (qz[0, 3] + qz[1, 3])
        else:
            wait_bytes(qr.at[j], qrecv.at[j])
            fin[:, n * LANE:(n + 1) * LANE] = own + jnp.sum(qr[j], axis=0)

    def meet(_):
        once(az, (0, 0, 4), (0, 1, 4))
        once(bx, *[(0, h, side, 1, 1) for h in (0, 1) for side in (0, 1)])

    def r2(j):
        r_send(j, 2)

    def r3(j):
        r_send(j, 3)

    def r4(j):
        r_send(j, 4)

    def a2(j):
        a_send(j, 2)

    def a3(j):
        a_send(j, 3)

    def a4(j):
        a_send(j, 4)

    def b2(j):
        b_second(j, 0)

    def b4(j):
        b_second(j, 1)

    cast(0, 0, 1)
    cast(1, 0, 1)
    pl.semaphore_wait(barrier, 7)
    send_far(0)
    send_far(1)
    stage(4)
    for j in (0, 1):
        cast(j, 1, NZ)
        send_rest(j)
    small[0].wait()
    hi, lo = split(bbuf[...].T)
    bth[...] = hi
    btl[...] = lo
    def flush(_):
        for cp in pending:
            cp.wait_send()
        pending.clear()
        small[1].wait()
        small[2].wait()

    order = (
        (a0, 0), (a0, 1), (stage, 5), (stage, 2), (stage, 3), (b1, 0), (a1, 0), (a2, 0), (stage, 6), (a1, 1),
        (a2, 1), (b1, 1), (a0, 2), (a0, 3), (a1, 2), (b2, 0), (a3, 0), (a1, 3), (b1, 2), (a3, 1), (a2, 2),
        (a4, 0), (b3, 0), (b2, 1), (a4, 1), (a2, 3), (b4, 0), (b2, 2), (a3, 2), (b3, 1), (a5, 0), (meet, 0),
        (b5, 0), (a5, 1), (a3, 3), (b3, 2), (a4, 2), (r2, 0), (b4, 1), (a4, 3), (a7, 0), (a7, 1), (b4, 2),
        (b5, 1), (a5, 2), (r3, 0), (a6, 1), (a6, 0), (b5, 2), (a5, 3), (r4, 0), (a6, 2), (b6, 1), (b6, 0),
        (flush, 0), (a6, 3), (b6, 2),
    )
    for step, j in order:
        step(j)

    acc = jnp.zeros((8, LANE), F32)
    for r in range(4):
        for j in range(7):
            v = fin[8 * r:8 * r + 8, LANE * j:LANE * (j + 1)]
            acc = acc + v * v

    ssq1[15] = acc
    spread(lambda k: ssq1.at[15], ssq1, nsend.at[0], nrecv.at[0], [((d + k) % 16, t) for k in range(1, 16)])
    wait_bytes(ssq1.at[0:15], nrecv.at[0])
    ssq2[15] = jnp.sum(ssq1[...], axis=0)
    spread(lambda k: ssq2.at[15], ssq2, nsend.at[1], nrecv.at[1], [(d, (t + k) % 16) for k in range(1, 16)])
    wait_bytes(ssq2.at[0:15], nrecv.at[1])
    squares = jnp.sum(jnp.sum(ssq2[...], axis=0), axis=0, keepdims=True)
    squares = jnp.sum(squares, axis=1, keepdims=True)
    limit = 0.25 * (R * FFW) ** 0.5
    factor = jnp.minimum(jnp.float32(1.0), limit / (jnp.sqrt(squares) + 1e-06))

    clipped = factor * fin[...]
    new_first = 0.9 * m1[...] + 0.1 * clipped
    new_second = 0.95 * m2[...] + 0.05 * clipped * clipped
    dirs[y, x] = new_first / (1.0 - 0.9**STEP) / (jnp.sqrt(new_second / (1.0 - 0.95**STEP)) + 1e-08)

    dx = {}
    firsts = (0, -1, 1, 2)
    sides = ((0, 1), (1, -1))

    def d_send(h, ring, hop, n, side, first, second, part):
        yo, xo = (second, first) if h == 0 else (first, second)
        ref = dirs.at[(y + yo + 4) % 4, (x + xo + 4) % 4, pl.ds(16 * h + part[0], part[1])]
        dx[h, ring, hop, n, side] = remote(
            ref, ref, dsend.at[h, ring, hop, n, side], drecv.at[h, ring, hop, n, side],
            toward(h, ring, sides[side][1]))

    def d_forward(n):
        for h in (0, 1):
            for side, sign in sides:
                dx[h, 1, 0, n, side].wait_recv()
                d_send(h, 1, 1, n, side, firsts[n], -sign, (8 * side, 8))

    for ring in (0, 1):
        for h in (0, 1):
            for side, _ in sides:
                d_send(h, ring, 0, 0, side, 0, 0, (0, 16))
    m1[...] = clipped
    out = pltpu.make_async_copy(m1, clipped_ref, lsem.at[1])
    out.start()
    for side, sign in sides:
        for h in (0, 1):
            dx[h, 0, 0, 0, side].wait_recv()
            d_send(h, 0, 1, 0, side, -sign, 0, (8 * side, 8))
            for other, _ in sides:
                d_send(h, 1, 0, 1 + side, other, -sign, 0, (0, 16))
    for j in (0, 1):
        wait_bytes(ah.at[j], hsend.at[j])
        wait_bytes(ar.at[j, 0:3], asend.at[j])
    for j in (2, 3):
        wait_bytes(ar.at[j], asend.at[j])
    for j in (1, 2):
        wait_bytes(qr.at[j], qsend.at[j])
    wait_bytes(ssq1.at[0:15], nsend.at[0])
    d_forward(0)
    for h in (0, 1):
        for side, _ in sides:
            dx[h, 0, 1, 0, side].wait_recv()
        for other, _ in sides:
            d_send(h, 1, 0, 3, other, 2, 0, (0, 16))
    for n in (1, 2, 3):
        d_forward(n)
    wait_bytes(ssq2.at[0:15], nsend.at[1])
    for n in range(4):
        for h in (0, 1):
            for side, _ in sides:
                dx[h, 1, 1, n, side].wait_recv()
    last = pltpu.make_async_copy(dirs, out_ref, lsem.at[2])
    last.start()
    for cp in pending:
        cp.wait_send()
    out.wait()
    last.wait()


def finish(
    dir_ref, clipped_ref, basis_ref, weight_ref, first_ref, second_ref,
    out_ref, out_first_ref, out_second_ref,
    dbuf, bbuf, wbuf, clipped, m1, m2, sem, osem,
):
    parts = ((0, 256), (256, 256), (512, 256), (768, 128))
    loads = [
        pltpu.make_async_copy(basis_ref, bbuf, sem.at[0]),
        pltpu.make_async_copy(clipped_ref, clipped, sem.at[1]),
        pltpu.make_async_copy(first_ref, m1, sem.at[2]),
        pltpu.make_async_copy(second_ref, m2, sem.at[3]),
    ]
    for n, (lo, width) in enumerate(parts):
        cols = pl.ds(lo, width)
        loads.append(pltpu.make_async_copy(dir_ref.at[:, cols], dbuf.at[:, cols], sem.at[4 + n]))
    for n, (lo, width) in enumerate(parts):
        cols = pl.ds(lo, width)
        loads.append(pltpu.make_async_copy(weight_ref.at[:, cols], wbuf.at[:, cols], sem.at[8 + n]))
    for cp in loads:
        cp.start()
    loads[0].wait()
    bh, bl = split(bbuf[...])
    for cp in loads[1:4]:
        cp.wait()
    m1[...] = 0.9 * m1[...] + 0.1 * clipped[...]
    m2[...] = 0.95 * m2[...] + 0.05 * clipped[...] * clipped[...]
    outs = [
        pltpu.make_async_copy(m1, out_first_ref, osem.at[0]),
        pltpu.make_async_copy(m2, out_second_ref, osem.at[1]),
    ]
    for cp in outs:
        cp.start()
    for n, (lo, width) in enumerate(parts):
        cols = slice(lo, lo + width)
        loads[4 + n].wait()
        loads[8 + n].wait()
        dh, dl = split(dbuf[:, cols])
        wbuf[:, cols] = wbuf[:, cols] - 0.5 * dot3(bh, bl, dh, dl)
        cp = pltpu.make_async_copy(wbuf.at[:, cols], out_ref.at[:, cols], osem.at[2 + n])
        cp.start()
        outs.append(cp)
    for cp in outs:
        cp.wait()


def body(grads, basis, weight, first_moment, second_moment):
    dma = pltpu.SemaphoreType.DMA
    vmem = pltpu.VMEM
    any_ = pl.BlockSpec(memory_space=pl.ANY)
    direction, clipped = pl.pallas_call(
        kernel,
        out_shape=(
            jax.ShapeDtypeStruct((4, 4, 32, OWN), F32),
            jax.ShapeDtypeStruct((32, OWN), F32),
        ),
        in_specs=[any_] * 4,
        out_specs=[any_] * 2,
        scratch_shapes=[
            vmem((2, 2, NZ, ROWS, 256), BF16),
            vmem((2, NZ, ROWS, NB * LANE), BF16),
            vmem((NA + NB, NZ, ROWS, LANE), F32),
            vmem((NA + NB, NZ, ROWS, LANE), F32),
            vmem((NA, 2, 4, ROWS, LANE), F32),
            vmem((NB, 4, 4, 32, 1024), F32),
            vmem((NB, 2, 2, 4, 32, 256), F32),
            vmem((NB, 2, 2, 4, 32, 512), F32),
            vmem((NB, 2, 2, 32, 256), F32),
            vmem((NB, 2, 2, 32, 512), F32),
            vmem((NB, NZ - 1, 32, LANE), F32),
            vmem((2, 4, 32, LANE), F32),
            vmem((NA, 4, 4, 32, LANE), F32),
            vmem((2, 3, 4, 32, LANE), F32),
            vmem((2, 4, 32, LANE), F32),
            vmem((NA, 15, 32, LANE), F32),
            vmem((32, OWN), F32),
            vmem((16, 8, LANE), F32),
            vmem((16, 8, LANE), F32),
            vmem((4, 4, 32, OWN), F32),
            vmem((32, OWN), F32),
            vmem((32, OWN), F32),
            vmem((ROWS, R), F32),
            vmem((R, ROWS), BF16),
            vmem((R, ROWS), BF16),
            dma((3, 2)),
            dma((3,)),
            dma((NA,)), dma((NA,)),
            dma((NA + NB,)), dma((NA + NB,)),
            dma((NA, 2, 4)), dma((NA, 2, 4)),
            dma((NA,)), dma((NA,)),
            dma((NB, 2, 2, 4)), dma((NB, 2, 2, 4)),
            dma((NB,)), dma((NB,)),
            dma((2,)), dma((2,)),
            dma((2, 4)), dma((2, 4)),
            dma((2,)), dma((2,)),
            dma((2, 2, 2, 4, 2)), dma((2, 2, 2, 4, 2)),
        ],
        compiler_params=pltpu.CompilerParams(
            collective_id=0, has_side_effects=True, vmem_limit_bytes=62 * 2**20),
        name="galore_step",
    )(grads[0], basis, first_moment, second_moment)
    return pl.pallas_call(
        finish,
        out_shape=(
            jax.ShapeDtypeStruct((ROWS, OWN), F32),
            jax.ShapeDtypeStruct((32, OWN), F32),
            jax.ShapeDtypeStruct((32, OWN), F32),
        ),
        in_specs=[any_] * 6,
        out_specs=[any_] * 3,
        scratch_shapes=[
            vmem((R, OWN), F32), vmem((ROWS, R), F32), vmem((ROWS, OWN), F32),
            vmem((32, OWN), F32), vmem((32, OWN), F32), vmem((32, OWN), F32),
            dma((12,)), dma((6,)),
        ],
        compiler_params=pltpu.CompilerParams(vmem_limit_bytes=62 * 2**20),
        name="galore_update",
    )(direction.reshape(R, OWN), clipped, basis, weight, first_moment, second_moment)


def solution(mesh):
    in_specs = (
        P("dp", "tensor", None),
        P("tensor", None),
        P("tensor", "dp"),
        P("tensor", "dp"),
        P("tensor", "dp"),
    )
    out_specs = (P("tensor", "dp"), P("tensor", "dp"), P("tensor", "dp"))
    return jax.shard_map(body, mesh=mesh, in_specs=in_specs, out_specs=out_specs, check_vma=False)
```

time: 119 us -> 96.4 us (0.81); the launches traced: 117 us -> 96.3 us
  Pallas kernels: 111 us -> 95.7 us
  local copies, waits for them, and re-layouts: 5.26 us -> 0 us
    pallas_call x1 -> x2, Pallas kernels: 111 us -> 95.7 us  [the longest x1 90.9 us: body(): pl.pallas_call(kernel, out_shape=(jax.ShapeDtypeStruct((4, 4, 32, OWN), F...]
    unnamed x3 -> x0, local copies, waits for them, and re-layouts: 5.26 us -> none
where the time goes in v2:
time: 96.4 us; the launch traced here: 96.3 us
  Pallas kernels  95.7 us (99%)
    pallas_call x1, Pallas kernels, body(): pl.pallas_call(kernel, out_shape=(jax.ShapeDtypeStruct((4, 4, 32, OWN), F...  90.9 us
    pallas_call x1, Pallas kernels, body(): pl.pallas_call(finish, out_shape=(jax.ShapeDtypeStruct((ROWS, OWN), F32),...  4.82 us

profile of v2, /device:TPU:4, one launch (start us, length us, event | category | flops | bytes accessed | tf_op | source)
XLA Modules:
  0.0 96.3 jit_solution(6418216094952650758)
XLA Ops:
  0.6 90.9 %galore_step.1 = (f32[4,4,32,896]{3,2,1,0:T(8,128)}, f32[32,896]{1,0:T(8,128)}) custom-call(bf16[256,14336]{1,0:T(8,128)(2,1)} %bitcast.2, f32[256,512]{1,0:T(8,128)} %basis_ref.3, f32[32,896]{1,0:T(8,128)} %first_ref.3, f32[32,896]{1,0:T(8,128)} %second_ref.3), custom_call_target="tpu_custom_call" | custom-call | tf_op jit(solution)/shard_map/galore_step/pallas_call | solution.py:529
  91.5 4.8 %galore_update.1 = (f32[256,896]{1,0:T(8,128)}, f32[32,896]{1,0:T(8,128)}, f32[32,896]{1,0:T(8,128)}) custom-call(f32[512,896]{1,0:T(8,128)} %bitcast.3, f32[32,896]{1,0:T(8,128)} %get-tuple-element.6.clipped_ref, f32[256,512]{1,0:T(8,128)} %basis_ref.3, f32[256,896]{1,0:T(8,128)} %weight_ref.1, f32[32,896]{1,0:T(8,128)} %first_ref.3, f32[32,896]{1,0:T(8,128)} %second_ref.3), custom_call_target="tpu_custom_call" | custom-call | tf_op jit(solution)/shard_map/galore_update/pallas_call | solution.py:580

commit v3 on v2

--- a/solution.py
+++ b/solution.py
@@ -35,7 +35,7 @@
     g_ref, basis_ref, first_ref, second_ref,
     out_ref, clipped_ref,
     ga, gb, cs, cr, zr, pb, rb1, rb2, rb3, rb4, qr, qz, pa, ah, hs, ar,
-    fin, ssq1, ssq2, dirs, m1, m2, bbuf, bth, btl,
+    fin, ssq1, ssq2, dirs, delta, m1, m2, bbuf, bth, btl, bh, bl,
     gsem, lsem, fsend, frecv, csend, crecv, zsend, zrecv, asend, arecv,
     bsend, brecv, qsend, qrecv, hsend, hrecv, rsend, rrecv, nsend, nrecv, dsend, drecv,
 ):
@@ -55,15 +55,22 @@
 
     partner = (z * 2 + 1 - c, t)
 
+    barrier = pltpu.get_barrier_semaphore()
+
+    for to in (at_z(1), at_z(-1), at_x(1), at_x(-1), at_y(1), at_y(-1), partner):
+        pl.semaphore_signal(barrier, 1, device_id=to, device_id_type=MESH)
+
     def gload(group, which, start):
         core = c if which == 0 else 1 - c
-        if group < 2:
-            buf, lo, width = ga.at[which, group], 256 * group, 256
+        first, last = (1, NZ) if group == 0 else (0, 1) if group == 3 else (0, NZ)
+        if group != 2:
+            buf, lo, width = ga.at[which, group % 3], 256 * (group % 3), 256
         else:
             buf, lo, width = gb.at[which], NA * LANE, NB * LANE
         sem = gsem.at[group, which]
         if not start:
-            pltpu.make_async_copy(buf, buf, sem).wait()
+            part = buf.at[first:last]
+            pltpu.make_async_copy(part, part, sem).wait()
             return
 
         def one(k, _):
@@ -71,27 +78,24 @@
             pltpu.make_async_copy(g_ref.at[:, pl.ds(col, width)], buf.at[k], sem).start()
             return 0
 
-        lax.fori_loop(0, NZ, one, 0)
+        lax.fori_loop(first, last, one, 0)
 
     small = [
         pltpu.make_async_copy(basis_ref, bbuf, lsem.at[0]),
         pltpu.make_async_copy(first_ref, m1, lsem.at[1]),
         pltpu.make_async_copy(second_ref, m2, lsem.at[2]),
     ]
+    gload(3, 1, True)
+    gload(3, 0, True)
+    gload(2, 1, True)
     gload(0, 1, True)
-    gload(2, 1, True)
+    small[0].start()
     gload(0, 0, True)
-    small[0].start()
     gload(2, 0, True)
     gload(1, 1, True)
     gload(1, 0, True)
     for cp in small[1:]:
         cp.start()
-
-    barrier = pltpu.get_barrier_semaphore()
-
-    for to in (at_z(1), at_z(-1), at_x(1), at_x(-1), at_y(1), at_y(-1), partner):
-        pl.semaphore_signal(barrier, 1, device_id=to, device_id_type=MESH)
 
     pending = []
 
@@ -111,17 +115,18 @@
             return ga[which, j // 2, k, :, (j % 2) * LANE:(j % 2 + 1) * LANE].astype(F32)
         return gb[which, k, :, (j - NA) * LANE:(j - NA + 1) * LANE].astype(F32)
 
-    def need(j, which):
+    def need(j, which, far_only=False):
         group = j // 2 if j < NA else 2
-        if (group, which) not in loaded:
-            loaded.add((group, which))
-            gload(group, which, False)
+        for part in (3,) if far_only and group == 0 else (3, 0) if group == 0 else (group,):
+            if (part, which) not in loaded:
+                loaded.add((part, which))
+                gload(part, which, False)
 
     core = {}
     far = {}
 
     def cast(j, lo, hi):
-        need(j, 1)
+        need(j, 1, hi == 1)
 
         def one(k, _):
             cs[j, k] = grad(j, 1, k)
@@ -171,12 +176,13 @@
                 zsend.at[j, side, s - 1], zrecv.at[j, side, s - 1], at_z(sign))
 
     def a0(j):
-        need(j, 0)
+        need(j, 0, True)
         far[j].wait_recv()
         cr[j, 0] = cr[j, 0] + grad(j, 0, 0)
         a_send(j, 1)
 
     def a1(j):
+        need(j, 0)
         core[j].wait_recv()
 
         def one(k, _):
@@ -365,33 +371,98 @@
     def b4(j):
         b_second(j, 1)
 
+    firsts = (0, -1, 1, 2)
+    sides = ((0, 1), (1, -1))
+
+    def gather(buf):
+        dx = {}
+
+        def send(h, ring, hop, n, side, first, second, part):
+            yo, xo = (second, first) if h == 0 else (first, second)
+            ref = buf.at[(y + yo + 4) % 4, (x + xo + 4) % 4, pl.ds(16 * h + part[0], part[1])]
+            dx[h, ring, hop, n, side] = remote(
+                ref, ref, dsend.at[h, ring, hop, n, side], drecv.at[h, ring, hop, n, side],
+                toward(h, ring, sides[side][1]))
+
+        def forward(n):
+            for h in (0, 1):
+                for side, sign in sides:
+                    dx[h, 1, 0, n, side].wait_recv()
+                    send(h, 1, 1, n, side, firsts[n], -sign, (8 * side, 8))
+
+        def g0():
+            for ring in (0, 1):
+                for h in (0, 1):
+                    for side, _ in sides:
+                        send(h, ring, 0, 0, side, 0, 0, (0, 16))
+
+        def g1():
+            for side, sign in sides:
+                for h in (0, 1):
+                    dx[h, 0, 0, 0, side].wait_recv()
+                    send(h, 0, 1, 0, side, -sign, 0, (8 * side, 8))
+                    for other, _ in sides:
+                        send(h, 1, 0, 1 + side, other, -sign, 0, (0, 16))
+
+        def g2():
+            forward(0)
+
+        def g3():
+            for h in (0, 1):
+                for side, _ in sides:
+                    dx[h, 0, 1, 0, side].wait_recv()
+                for other, _ in sides:
+                    send(h, 1, 0, 3, other, 2, 0, (0, 16))
+
+        def g4():
+            forward(1)
+            forward(2)
+
+        def g5():
+            forward(3)
+
+        def close():
+            for n in range(4):
+                for h in (0, 1):
+                    for side, _ in sides:
+                        dx[h, 1, 1, n, side].wait_recv()
+
+        return g0, g1, g2, g3, g4, g5, close
+
     cast(0, 0, 1)
     cast(1, 0, 1)
     pl.semaphore_wait(barrier, 7)
     send_far(0)
     send_far(1)
     stage(4)
-    for j in (0, 1):
+
+    def rest(j):
         cast(j, 1, NZ)
         send_rest(j)
-    small[0].wait()
-    hi, lo = split(bbuf[...].T)
-    bth[...] = hi
-    btl[...] = lo
+
+    def prep(_):
+        small[0].wait()
+        hi, lo = split(bbuf[...].T)
+        bth[...] = hi
+        btl[...] = lo
+
     def flush(_):
         for cp in pending:
             cp.wait_send()
         pending.clear()
-        small[1].wait()
-        small[2].wait()
+        for cp in small[1:]:
+            cp.wait()
+        hi, lo = split(bbuf[...])
+        bh[...] = hi
+        bl[...] = lo
 
     order = (
-        (a0, 0), (a0, 1), (stage, 5), (stage, 2), (stage, 3), (b1, 0), (a1, 0), (a2, 0), (stage, 6), (a1, 1),
-        (a2, 1), (b1, 1), (a0, 2), (a0, 3), (a1, 2), (b2, 0), (a3, 0), (a1, 3), (b1, 2), (a3, 1), (a2, 2),
-        (a4, 0), (b3, 0), (b2, 1), (a4, 1), (a2, 3), (b4, 0), (b2, 2), (a3, 2), (b3, 1), (a5, 0), (meet, 0),
-        (b5, 0), (a5, 1), (a3, 3), (b3, 2), (a4, 2), (r2, 0), (b4, 1), (a4, 3), (a7, 0), (a7, 1), (b4, 2),
-        (b5, 1), (a5, 2), (r3, 0), (a6, 1), (a6, 0), (b5, 2), (a5, 3), (r4, 0), (a6, 2), (b6, 1), (b6, 0),
-        (flush, 0), (a6, 3), (b6, 2),
+        (rest, 0), (prep, 0), (a0, 0), (a0, 1), (stage, 2), (stage, 6), (rest, 1), (b1, 0), (a0, 2), (a1, 0),
+        (a2, 0), (stage, 3), (stage, 5), (a1, 2), (a2, 2), (b1, 2), (a1, 1), (a2, 1), (a0, 3), (a1, 3),
+        (a3, 0), (b2, 0), (b1, 1), (a3, 2), (b2, 2), (a3, 1), (a2, 3), (b3, 0), (a4, 0), (b2, 1), (a4, 1),
+        (b3, 2), (a3, 3), (b4, 0), (a4, 2), (b3, 1), (b4, 2), (a5, 1), (a5, 0), (meet, 0), (b5, 0), (a4, 3),
+        (b4, 1), (r2, 0), (b5, 2), (a5, 2), (a5, 3), (r3, 0), (b5, 1), (a7, 0), (a7, 1), (r4, 0), (b6, 2),
+        (a6, 2), (b6, 0), (a6, 0), (a6, 1), (flush, 0), (a6, 3), (b6, 1),
     )
     for step, j in order:
         step(j)
@@ -417,37 +488,16 @@
     new_first = 0.9 * m1[...] + 0.1 * clipped
     new_second = 0.95 * m2[...] + 0.05 * clipped * clipped
     dirs[y, x] = new_first / (1.0 - 0.9**STEP) / (jnp.sqrt(new_second / (1.0 - 0.95**STEP)) + 1e-08)
-
-    dx = {}
-    firsts = (0, -1, 1, 2)
-    sides = ((0, 1), (1, -1))
-
-    def d_send(h, ring, hop, n, side, first, second, part):
-        yo, xo = (second, first) if h == 0 else (first, second)
-        ref = dirs.at[(y + yo + 4) % 4, (x + xo + 4) % 4, pl.ds(16 * h + part[0], part[1])]
-        dx[h, ring, hop, n, side] = remote(
-            ref, ref, dsend.at[h, ring, hop, n, side], drecv.at[h, ring, hop, n, side],
-            toward(h, ring, sides[side][1]))
-
-    def d_forward(n):
-        for h in (0, 1):
-            for side, sign in sides:
-                dx[h, 1, 0, n, side].wait_recv()
-                d_send(h, 1, 1, n, side, firsts[n], -sign, (8 * side, 8))
-
-    for ring in (0, 1):
-        for h in (0, 1):
-            for side, _ in sides:
-                d_send(h, ring, 0, 0, side, 0, 0, (0, 16))
-    m1[...] = clipped
-    out = pltpu.make_async_copy(m1, clipped_ref, lsem.at[1])
-    out.start()
-    for side, sign in sides:
-        for h in (0, 1):
-            dx[h, 0, 0, 0, side].wait_recv()
-            d_send(h, 0, 1, 0, side, -sign, 0, (8 * side, 8))
-            for other, _ in sides:
-                d_send(h, 1, 0, 1 + side, other, -sign, 0, (0, 16))
+    d0, d1, d2, d3, d4, d5, direction_here = gather(dirs)
+    d0()
+    fin[...] = clipped
+    outs = [pltpu.make_async_copy(fin, clipped_ref, lsem.at[0])]
+    outs[0].start()
+
+    d1()
+    d2()
+    d3()
+    d4()
     for j in (0, 1):
         wait_bytes(ah.at[j], hsend.at[j])
         wait_bytes(ar.at[j, 0:3], asend.at[j])
@@ -456,68 +506,51 @@
     for j in (1, 2):
         wait_bytes(qr.at[j], qsend.at[j])
     wait_bytes(ssq1.at[0:15], nsend.at[0])
-    d_forward(0)
-    for h in (0, 1):
-        for side, _ in sides:
-            dx[h, 0, 1, 0, side].wait_recv()
-        for other, _ in sides:
-            d_send(h, 1, 0, 3, other, 2, 0, (0, 16))
-    for n in (1, 2, 3):
-        d_forward(n)
     wait_bytes(ssq2.at[0:15], nsend.at[1])
-    for n in range(4):
-        for h in (0, 1):
-            for side, _ in sides:
-                dx[h, 1, 1, n, side].wait_recv()
-    last = pltpu.make_async_copy(dirs, out_ref, lsem.at[2])
-    last.start()
+    d5()
+    direction_here()
+    for n, (lo_col, width) in enumerate(((0, 256), (256, 256), (512, 256), (768, 128))):
+        cols = slice(lo_col, lo_col + width)
+        hi, lo = split(dirs[:, :, :, cols].reshape(R, width))
+        delta[:, cols] = dot3(bh[...], bl[...], hi, lo)
+        outs.append(pltpu.make_async_copy(delta.at[:, cols], out_ref.at[:, cols], lsem.at[1 + n]))
+        outs[-1].start()
     for cp in pending:
         cp.wait_send()
-    out.wait()
-    last.wait()
+    for cp in outs:
+        cp.wait()
 
 
 def finish(
-    dir_ref, clipped_ref, basis_ref, weight_ref, first_ref, second_ref,
+    delta_ref, clipped_ref, weight_ref, first_ref, second_ref,
     out_ref, out_first_ref, out_second_ref,
-    dbuf, bbuf, wbuf, clipped, m1, m2, sem, osem,
+    dbuf, wbuf, clipped, m1, m2, sem, osem,
 ):
-    parts = ((0, 256), (256, 256), (512, 256), (768, 128))
-    loads = [
-        pltpu.make_async_copy(basis_ref, bbuf, sem.at[0]),
-        pltpu.make_async_copy(clipped_ref, clipped, sem.at[1]),
-        pltpu.make_async_copy(first_ref, m1, sem.at[2]),
-        pltpu.make_async_copy(second_ref, m2, sem.at[3]),
-    ]
-    for n, (lo, width) in enumerate(parts):
-        cols = pl.ds(lo, width)
-        loads.append(pltpu.make_async_copy(dir_ref.at[:, cols], dbuf.at[:, cols], sem.at[4 + n]))
-    for n, (lo, width) in enumerate(parts):
-        cols = pl.ds(lo, width)
-        loads.append(pltpu.make_async_copy(weight_ref.at[:, cols], wbuf.at[:, cols], sem.at[8 + n]))
+    loads = []
+    for n in range(4):
+        rows = pl.ds(64 * n, 64)
+        loads.append(pltpu.make_async_copy(weight_ref.at[rows], wbuf.at[rows], sem.at[2 * n]))
+        loads.append(pltpu.make_async_copy(delta_ref.at[rows], dbuf.at[rows], sem.at[2 * n + 1]))
+    loads.append(pltpu.make_async_copy(clipped_ref, clipped, sem.at[8]))
+    loads.append(pltpu.make_async_copy(first_ref, m1, sem.at[9]))
+    loads.append(pltpu.make_async_copy(second_ref, m2, sem.at[10]))
     for cp in loads:
         cp.start()
-    loads[0].wait()
-    bh, bl = split(bbuf[...])
-    for cp in loads[1:4]:
+    outs = []
+    for n in range(4):
+        rows = slice(64 * n, 64 * n + 64)
+        loads[2 * n].wait()
+        loads[2 * n + 1].wait()
+        wbuf[rows] = wbuf[rows] - 0.5 * dbuf[rows]
+        outs.append(pltpu.make_async_copy(wbuf.at[rows], out_ref.at[rows], osem.at[n]))
+        outs[-1].start()
+    for cp in loads[8:]:
         cp.wait()
     m1[...] = 0.9 * m1[...] + 0.1 * clipped[...]
     m2[...] = 0.95 * m2[...] + 0.05 * clipped[...] * clipped[...]
-    outs = [
-        pltpu.make_async_copy(m1, out_first_ref, osem.at[0]),
-        pltpu.make_async_copy(m2, out_second_ref, osem.at[1]),
-    ]
-    for cp in outs:
-        cp.start()
-    for n, (lo, width) in enumerate(parts):
-        cols = slice(lo, lo + width)
-        loads[4 + n].wait()
-        loads[8 + n].wait()
-        dh, dl = split(dbuf[:, cols])
-        wbuf[:, cols] = wbuf[:, cols] - 0.5 * dot3(bh, bl, dh, dl)
-        cp = pltpu.make_async_copy(wbuf.at[:, cols], out_ref.at[:, cols], osem.at[2 + n])
-        cp.start()
-        outs.append(cp)
+    for n, (src, dst) in enumerate(((m1, out_first_ref), (m2, out_second_ref))):
+        outs.append(pltpu.make_async_copy(src, dst, osem.at[4 + n]))
+        outs[-1].start()
     for cp in outs:
         cp.wait()
 
@@ -526,10 +559,10 @@
     dma = pltpu.SemaphoreType.DMA
     vmem = pltpu.VMEM
     any_ = pl.BlockSpec(memory_space=pl.ANY)
-    direction, clipped = pl.pallas_call(
+    delta, clipped = pl.pallas_call(
         kernel,
         out_shape=(
-            jax.ShapeDtypeStruct((4, 4, 32, OWN), F32),
+            jax.ShapeDtypeStruct((ROWS, OWN), F32),
             jax.ShapeDtypeStruct((32, OWN), F32),
         ),
         in_specs=[any_] * 4,
@@ -555,13 +588,16 @@
             vmem((16, 8, LANE), F32),
             vmem((16, 8, LANE), F32),
             vmem((4, 4, 32, OWN), F32),
+            vmem((ROWS, OWN), F32),
             vmem((32, OWN), F32),
             vmem((32, OWN), F32),
             vmem((ROWS, R), F32),
             vmem((R, ROWS), BF16),
             vmem((R, ROWS), BF16),
-            dma((3, 2)),
-            dma((3,)),
+            vmem((ROWS, R), BF16),
+            vmem((ROWS, R), BF16),
+            dma((4, 2)),
+            dma((5,)),
             dma((NA,)), dma((NA,)),
             dma((NA + NB,)), dma((NA + NB,)),
             dma((NA, 2, 4)), dma((NA, 2, 4)),
@@ -584,16 +620,16 @@
             jax.ShapeDtypeStruct((32, OWN), F32),
             jax.ShapeDtypeStruct((32, OWN), F32),
         ),
-        in_specs=[any_] * 6,
+        in_specs=[any_] * 5,
         out_specs=[any_] * 3,
         scratch_shapes=[
-            vmem((R, OWN), F32), vmem((ROWS, R), F32), vmem((ROWS, OWN), F32),
+            vmem((ROWS, OWN), F32), vmem((ROWS, OWN), F32),
             vmem((32, OWN), F32), vmem((32, OWN), F32), vmem((32, OWN), F32),
-            dma((12,)), dma((6,)),
+            dma((11,)), dma((6,)),
         ],
         compiler_params=pltpu.CompilerParams(vmem_limit_bytes=62 * 2**20),
         name="galore_update",
-    )(direction.reshape(R, OWN), clipped, basis, weight, first_moment, second_moment)
+    )(delta, clipped, weight, first_moment, second_moment)
 
 
 def solution(mesh):

time: 96.4 us -> 93.1 us (0.966)
  Pallas kernels: 95.7 us -> 92.3 us
    pallas_call x1, Pallas kernels: 4.82 us -> 2.52 us  [body(): pl.pallas_call(finish, out_shape=(jax.ShapeDtypeStruct((ROWS, OWN), F32),...]
    pallas_call x1, Pallas kernels: 90.9 us -> 89.8 us  [body(): pl.pallas_call(kernel, out_shape=(jax.ShapeDtypeStruct((ROWS, OWN), F32),...]
where the time goes in v3:
time: 93.1 us; the launch traced here: 92.9 us
  Pallas kernels  92.3 us (99%)
    pallas_call x1, Pallas kernels, body(): pl.pallas_call(kernel, out_shape=(jax.ShapeDtypeStruct((ROWS, OWN), F32),...  89.8 us
    pallas_call x1, Pallas kernels, body(): pl.pallas_call(finish, out_shape=(jax.ShapeDtypeStruct((ROWS, OWN), F32),...  2.52 us

profile of v3, /device:TPU:4, one launch (start us, length us, event | category | flops | bytes accessed | tf_op | source)
XLA Modules:
  0.0 92.9 jit_solution(9820701048190003385)
XLA Ops:
  0.6 89.8 %galore_step.1 = (f32[256,896]{1,0:T(8,128)}, f32[32,896]{1,0:T(8,128)}) custom-call(bf16[256,14336]{1,0:T(8,128)(2,1)} %bitcast.1, f32[256,512]{1,0:T(8,128)} %basis_ref.1, f32[32,896]{1,0:T(8,128)} %first_ref.3, f32[32,896]{1,0:T(8,128)} %second_ref.3), custom_call_target="tpu_custom_call" | custom-call | tf_op jit(solution)/shard_map/galore_step/pallas_call | solution.py:562
  90.4 2.5 %galore_update.1 = (f32[256,896]{1,0:T(8,128)}, f32[32,896]{1,0:T(8,128)}, f32[32,896]{1,0:T(8,128)}) custom-call(f32[256,896]{1,0:T(8,128)} %get-tuple-element.5.delta_ref, f32[32,896]{1,0:T(8,128)} %get-tuple-element.6.clipped_ref, f32[256,896]{1,0:T(8,128)} %weight_ref.1, f32[32,896]{1,0:T(8,128)} %first_ref.3, f32[32,896]{1,0:T(8,128)} %second_ref.3), custom_call_target="tpu_custom_call" | custom-call | tf_op jit(solution)/shard_map/galore_update/pallas_call | solution.py:616

commit v4 on v3

--- a/solution.py
+++ b/solution.py
@@ -384,42 +384,31 @@
                 ref, ref, dsend.at[h, ring, hop, n, side], drecv.at[h, ring, hop, n, side],
                 toward(h, ring, sides[side][1]))
 
-        def forward(n):
+        def own():
+            for ring in (0, 1):
+                for h in (0, 1):
+                    for side, _ in sides:
+                        send(h, ring, 0, 0, side, 0, 0, (0, 16))
+
+        def first_halves():
+            for side, sign in sides:
+                for h in (0, 1):
+                    dx[h, 0, 0, 0, side].wait_recv()
+                    send(h, 0, 1, 0, side, -sign, 0, (8 * side, 8))
+
+        def second(n):
+            for h in (0, 1):
+                if n == 3:
+                    for side, _ in sides:
+                        dx[h, 0, 1, 0, side].wait_recv()
+                for side, _ in sides:
+                    send(h, 1, 0, n, side, firsts[n], 0, (0, 16))
+
+        def second_halves(n):
             for h in (0, 1):
                 for side, sign in sides:
                     dx[h, 1, 0, n, side].wait_recv()
                     send(h, 1, 1, n, side, firsts[n], -sign, (8 * side, 8))
-
-        def g0():
-            for ring in (0, 1):
-                for h in (0, 1):
-                    for side, _ in sides:
-                        send(h, ring, 0, 0, side, 0, 0, (0, 16))
-
-        def g1():
-            for side, sign in sides:
-                for h in (0, 1):
-                    dx[h, 0, 0, 0, side].wait_recv()
-                    send(h, 0, 1, 0, side, -sign, 0, (8 * side, 8))
-                    for other, _ in sides:
-                        send(h, 1, 0, 1 + side, other, -sign, 0, (0, 16))
-
-        def g2():
-            forward(0)
-
-        def g3():
-            for h in (0, 1):
-                for side, _ in sides:
-                    dx[h, 0, 1, 0, side].wait_recv()
-                for other, _ in sides:
-                    send(h, 1, 0, 3, other, 2, 0, (0, 16))
-
-        def g4():
-            forward(1)
-            forward(2)
-
-        def g5():
-            forward(3)
 
         def close():
             for n in range(4):
@@ -427,7 +416,7 @@
                     for side, _ in sides:
                         dx[h, 1, 1, n, side].wait_recv()
 
-        return g0, g1, g2, g3, g4, g5, close
+        return own, first_halves, second, second_halves, close
 
     cast(0, 0, 1)
     cast(1, 0, 1)
@@ -457,12 +446,12 @@
         bl[...] = lo
 
     order = (
-        (rest, 0), (prep, 0), (a0, 0), (a0, 1), (stage, 2), (stage, 6), (rest, 1), (b1, 0), (a0, 2), (a1, 0),
-        (a2, 0), (stage, 3), (stage, 5), (a1, 2), (a2, 2), (b1, 2), (a1, 1), (a2, 1), (a0, 3), (a1, 3),
-        (a3, 0), (b2, 0), (b1, 1), (a3, 2), (b2, 2), (a3, 1), (a2, 3), (b3, 0), (a4, 0), (b2, 1), (a4, 1),
-        (b3, 2), (a3, 3), (b4, 0), (a4, 2), (b3, 1), (b4, 2), (a5, 1), (a5, 0), (meet, 0), (b5, 0), (a4, 3),
-        (b4, 1), (r2, 0), (b5, 2), (a5, 2), (a5, 3), (r3, 0), (b5, 1), (a7, 0), (a7, 1), (r4, 0), (b6, 2),
-        (a6, 2), (b6, 0), (a6, 0), (a6, 1), (flush, 0), (a6, 3), (b6, 1),
+        (rest, 1), (stage, 5), (a0, 1), (a0, 0), (rest, 0), (stage, 3), (prep, 0), (b1, 0), (a1, 1), (a2, 1),
+        (stage, 6), (b1, 1), (a1, 0), (a2, 0), (stage, 2), (a1, 3), (b2, 0), (a0, 2), (a0, 3), (b1, 2),
+        (a1, 2), (a3, 0), (a2, 2), (a3, 1), (a2, 3), (b3, 0), (b2, 1), (b2, 2), (a3, 2), (b4, 0), (a4, 0),
+        (b3, 1), (a4, 2), (a3, 3), (b3, 2), (meet, 0), (b5, 0), (a4, 1), (b4, 1), (a5, 2), (b4, 2), (a5, 0),
+        (r2, 0), (a4, 3), (a5, 1), (r3, 0), (b5, 1), (b5, 2), (a6, 2), (a5, 3), (r4, 0), (a7, 0), (a7, 1),
+        (b6, 1), (b6, 0), (a6, 1), (a6, 0), (flush, 0), (a6, 3), (b6, 2),
     )
     for step, j in order:
         step(j)
@@ -488,16 +477,17 @@
     new_first = 0.9 * m1[...] + 0.1 * clipped
     new_second = 0.95 * m2[...] + 0.05 * clipped * clipped
     dirs[y, x] = new_first / (1.0 - 0.9**STEP) / (jnp.sqrt(new_second / (1.0 - 0.95**STEP)) + 1e-08)
-    d0, d1, d2, d3, d4, d5, direction_here = gather(dirs)
-    d0()
+    own, first_halves, second, second_halves, close = gather(dirs)
+    own()
     fin[...] = clipped
     outs = [pltpu.make_async_copy(fin, clipped_ref, lsem.at[0])]
     outs[0].start()
 
-    d1()
-    d2()
-    d3()
-    d4()
+    first_halves()
+    for n in (1, 2, 3):
+        second(n)
+    for n in (0, 1, 2):
+        second_halves(n)
     for j in (0, 1):
         wait_bytes(ah.at[j], hsend.at[j])
         wait_bytes(ar.at[j, 0:3], asend.at[j])
@@ -507,8 +497,8 @@
         wait_bytes(qr.at[j], qsend.at[j])
     wait_bytes(ssq1.at[0:15], nsend.at[0])
     wait_bytes(ssq2.at[0:15], nsend.at[1])
-    d5()
-    direction_here()
+    second_halves(3)
+    close()
     for n, (lo_col, width) in enumerate(((0, 256), (256, 256), (512, 256), (768, 128))):
         cols = slice(lo_col, lo_col + width)
         hi, lo = split(dirs[:, :, :, cols].reshape(R, width))

time: 93.1 us -> 91.8 us (0.986); the launches traced: 92.9 us -> 90.6 us
  Pallas kernels: 92.3 us -> 90 us
    pallas_call x1, Pallas kernels: 89.8 us -> 87.5 us  [body(): pl.pallas_call(kernel, out_shape=(jax.ShapeDtypeStruct((ROWS, OWN), F32),...]
where the time goes in v4:
time: 91.8 us; the launch traced here: 90.6 us
  Pallas kernels  90 us (98%)
    pallas_call x1, Pallas kernels, body(): pl.pallas_call(kernel, out_shape=(jax.ShapeDtypeStruct((ROWS, OWN), F32),...  87.5 us
    pallas_call x1, Pallas kernels, body(): pl.pallas_call(finish, out_shape=(jax.ShapeDtypeStruct((ROWS, OWN), F32),...  2.52 us

profile of v4, /device:TPU:4, one launch (start us, length us, event | category | flops | bytes accessed | tf_op | source)
XLA Modules:
  0.0 90.6 jit_solution(6716839411641230874)
XLA Ops:
  0.6 87.5 %galore_step.1 = (f32[256,896]{1,0:T(8,128)}, f32[32,896]{1,0:T(8,128)}) custom-call(bf16[256,14336]{1,0:T(8,128)(2,1)} %bitcast.1, f32[256,512]{1,0:T(8,128)} %basis_ref.1, f32[32,896]{1,0:T(8,128)} %first_ref.3, f32[32,896]{1,0:T(8,128)} %second_ref.3), custom_call_target="tpu_custom_call" | custom-call | tf_op jit(solution)/shard_map/galore_step/pallas_call | solution.py:552
  88.1 2.5 %galore_update.1 = (f32[256,896]{1,0:T(8,128)}, f32[32,896]{1,0:T(8,128)}, f32[32,896]{1,0:T(8,128)}) custom-call(f32[256,896]{1,0:T(8,128)} %get-tuple-element.5.delta_ref, f32[32,896]{1,0:T(8,128)} %get-tuple-element.6.clipped_ref, f32[256,896]{1,0:T(8,128)} %weight_ref.1, f32[32,896]{1,0:T(8,128)} %first_ref.3, f32[32,896]{1,0:T(8,128)} %second_ref.3), custom_call_target="tpu_custom_call" | custom-call | tf_op jit(solution)/shard_map/galore_update/pallas_call | solution.py:606

commit v5 on v4

--- a/solution.py
+++ b/solution.py
@@ -516,30 +516,33 @@
     out_ref, out_first_ref, out_second_ref,
     dbuf, wbuf, clipped, m1, m2, sem, osem,
 ):
-    loads = []
+    loads = [
+        pltpu.make_async_copy(clipped_ref, clipped, sem.at[8]),
+        pltpu.make_async_copy(first_ref, m1, sem.at[9]),
+        pltpu.make_async_copy(second_ref, m2, sem.at[10]),
+    ]
     for n in range(4):
         rows = pl.ds(64 * n, 64)
         loads.append(pltpu.make_async_copy(weight_ref.at[rows], wbuf.at[rows], sem.at[2 * n]))
         loads.append(pltpu.make_async_copy(delta_ref.at[rows], dbuf.at[rows], sem.at[2 * n + 1]))
-    loads.append(pltpu.make_async_copy(clipped_ref, clipped, sem.at[8]))
-    loads.append(pltpu.make_async_copy(first_ref, m1, sem.at[9]))
-    loads.append(pltpu.make_async_copy(second_ref, m2, sem.at[10]))
     for cp in loads:
         cp.start()
-    outs = []
-    for n in range(4):
-        rows = slice(64 * n, 64 * n + 64)
-        loads[2 * n].wait()
-        loads[2 * n + 1].wait()
-        wbuf[rows] = wbuf[rows] - 0.5 * dbuf[rows]
-        outs.append(pltpu.make_async_copy(wbuf.at[rows], out_ref.at[rows], osem.at[n]))
-        outs[-1].start()
-    for cp in loads[8:]:
+    for cp in loads[0:3]:
         cp.wait()
     m1[...] = 0.9 * m1[...] + 0.1 * clipped[...]
     m2[...] = 0.95 * m2[...] + 0.05 * clipped[...] * clipped[...]
-    for n, (src, dst) in enumerate(((m1, out_first_ref), (m2, out_second_ref))):
-        outs.append(pltpu.make_async_copy(src, dst, osem.at[4 + n]))
+    outs = [
+        pltpu.make_async_copy(m1, out_first_ref, osem.at[4]),
+        pltpu.make_async_copy(m2, out_second_ref, osem.at[5]),
+    ]
+    for cp in outs:
+        cp.start()
+    for n in range(4):
+        rows = slice(64 * n, 64 * n + 64)
+        loads[3 + 2 * n].wait()
+        loads[4 + 2 * n].wait()
+        wbuf[rows] = wbuf[rows] - 0.5 * dbuf[rows]
+        outs.append(pltpu.make_async_copy(wbuf.at[rows], out_ref.at[rows], osem.at[n]))
         outs[-1].start()
     for cp in outs:
         cp.wait()

time: 91.8 us -> 91.8 us (level)
  no operation moved by 1% of the time
where the time goes in v5:
time: 91.8 us; the launch traced here: 90.6 us
  Pallas kernels  90 us (98%)
    pallas_call x1, Pallas kernels, body(): pl.pallas_call(kernel, out_shape=(jax.ShapeDtypeStruct((ROWS, OWN), F32),...  87.5 us
    pallas_call x1, Pallas kernels, body(): pl.pallas_call(finish, out_shape=(jax.ShapeDtypeStruct((ROWS, OWN), F32),...  2.5 us

profile of v5, /device:TPU:4, one launch (start us, length us, event | category | flops | bytes accessed | tf_op | source)
XLA Modules:
  0.0 90.6 jit_solution(7606322237343967655)
XLA Ops:
  0.6 87.5 %galore_step.1 = (f32[256,896]{1,0:T(8,128)}, f32[32,896]{1,0:T(8,128)}) custom-call(bf16[256,14336]{1,0:T(8,128)(2,1)} %bitcast.1, f32[256,512]{1,0:T(8,128)} %basis_ref.1, f32[32,896]{1,0:T(8,128)} %first_ref.3, f32[32,896]{1,0:T(8,128)} %second_ref.3), custom_call_target="tpu_custom_call" | custom-call | tf_op jit(solution)/shard_map/galore_step/pallas_call | solution.py:555
  88.1 2.5 %galore_update.1 = (f32[256,896]{1,0:T(8,128)}, f32[32,896]{1,0:T(8,128)}, f32[32,896]{1,0:T(8,128)}) custom-call(f32[256,896]{1,0:T(8,128)} %get-tuple-element.5.delta_ref, f32[32,896]{1,0:T(8,128)} %get-tuple-element.6.clipped_ref, f32[256,896]{1,0:T(8,128)} %weight_ref.1, f32[32,896]{1,0:T(8,128)} %first_ref.3, f32[32,896]{1,0:T(8,128)} %second_ref.3), custom_call_target="tpu_custom_call" | custom-call | tf_op jit(solution)/shard_map/galore_update/pallas_call | solution.py:609
